TPU v7x, 512 devices: a whole 4x4x16 slice. The times are simulated.
512 devices in a mesh: blk: 64 (over z, y_lo, core), rows: 8 (over y_hi, x).
Axes of the slice: x: 4, y: 4 (y_hi: 2, y_lo: 2; y = y_hi * 2 + y_lo), z: 16, core: 2. Of those that a mesh axis runs over, the one named last changes fastest.
Arguments:
- blocks: bfloat16 [64, 8, 3, 64, 4096], P('blk', 'rows'), may hold values from -6 to 6
- block_row: int32 [64, 8, 3], P('blk', 'rows'), may hold values from 0 to 7
- block_col: int32 [64, 8, 3], P('blk', 'rows'), may hold values from 0 to 63
- block_ctx: int32 [64, 8, 3], P('blk', 'rows'), may hold values from 0 to 1
- live_blocks: int32 [64, 8], P('blk', 'rows'), may hold values from 1 to 3, as said below
- user_factor: float32 [32768, 256], P(('blk', 'rows')), may hold values from -2.5 to 2.5
- item_factor: float32 [4096, 256], P('blk'), may hold values from -2.5 to 2.5
- context_factor: float32 [128, 256], replicated, may hold values from -2.5 to 2.5
Outputs:
- new_users: float32 [32768, 256], P(('blk', 'rows'))
- new_items: float32 [4096, 256], P('blk')
- context_grad: float32 [128, 256], replicated
Inputs may be any that keep to these rules, and one draw needn't show every extreme that they name: `live_blocks`: every device has at least one used slot; in every draw some device uses all 3 slots.
All inputs are finite; a program needn't handle non-finite values.
Results may differ from a plain program's by a relative error of at most 0.0089.
The roundings to bfloat16 on the way count: a program that leaves them out, or rounds other values in their place, can miss the bound.
Values may be sent and summed in bfloat16 or wider, within the bound.
A program may use at most 64 MiB of HBM per device.

v0:
```python
import math

import jax
import jax.numpy as jnp
from jax import lax
from jax.sharding import PartitionSpec as P

ITERS = 2


def block_terms(block_x, user_rows, item_rows, context_rows, with_context):
    block_edge = user_rows.shape[0]
    factor_rank = user_rows.shape[1]
    user_wide = user_rows.astype(jnp.float32)
    item_wide = item_rows.astype(jnp.float32)
    context_wide = context_rows.astype(jnp.float32)
    pair_vw = (
        (item_wide[:, None, :] * context_wide[None, :, :])
        .astype(jnp.bfloat16)
        .reshape(block_edge * block_edge, factor_rank)
    )
    model_block = lax.dot_general(
        user_rows, pair_vw, (((1,), (1,)), ((), ())), preferred_element_type=jnp.float32
    )
    residual = (model_block - block_x.astype(jnp.float32)).astype(jnp.bfloat16)
    user_term = jnp.dot(residual, pair_vw, preferred_element_type=jnp.float32)
    pair_uw = (
        (user_wide[:, None, :] * context_wide[None, :, :])
        .astype(jnp.bfloat16)
        .reshape(block_edge * block_edge, factor_rank)
    )
    resid_items = (
        residual.reshape(block_edge, block_edge, block_edge)
        .transpose(1, 0, 2)
        .reshape(block_edge, block_edge * block_edge)
    )
    item_term = jnp.dot(resid_items, pair_uw, preferred_element_type=jnp.float32)
    if with_context:
        pair_uv = (
            (user_wide[:, None, :] * item_wide[None, :, :])
            .astype(jnp.bfloat16)
            .reshape(block_edge * block_edge, factor_rank)
        )
        context_term = lax.dot_general(
            residual.reshape(block_edge * block_edge, block_edge),
            pair_uv,
            (((0,), (0,)), ((), ())),
            preferred_element_type=jnp.float32,
        )
    else:
        context_term = jnp.zeros((block_edge, factor_rank), jnp.float32)
    return (user_term, item_term, context_term)


def add_rows(target, start_row, term):
    current = lax.dynamic_slice_in_dim(target, start_row, term.shape[0], 0)
    return lax.dynamic_update_slice_in_dim(target, current + term, start_row, 0)


def local(
    blocks, block_row, block_col, block_ctx, live_blocks, user_factor, item_factor, context_factor
):
    block_edge = blocks.shape[3]
    factor_rank = user_factor.shape[1]
    slot_count = blocks.shape[2]
    slot_blocks = blocks[0, 0]
    rows_of = block_row[0, 0]
    items_of = block_col[0, 0]
    contexts_of = block_ctx[0, 0]
    live_count = live_blocks[0, 0]
    row_groups = lax.axis_size("rows")
    blk_count = lax.axis_size("blk")
    user_step = 6.4 / (block_edge * block_edge)
    item_step = 16.0 / (block_edge * block_edge * row_groups)
    grad_scale = 8.0 / (block_edge * math.sqrt(blk_count * row_groups))
    context_bf = context_factor.astype(jnp.bfloat16)
    context_grad = jnp.zeros(context_factor.shape, jnp.float32)
    for step_index in range(ITERS):
        is_last = step_index == ITERS - 1
        group_users = lax.all_gather(user_factor.astype(jnp.bfloat16), "rows", axis=0, tiled=True)
        all_items = lax.all_gather(item_factor.astype(jnp.bfloat16), "blk", axis=0, tiled=True)

        def visit_block(slot_index, carried):
            user_acc, item_acc, ctx_acc, item_tiles = carried
            block_x = lax.dynamic_index_in_dim(slot_blocks, slot_index, 0, keepdims=False)
            row_at = rows_of[slot_index] * block_edge
            item_at = items_of[slot_index] * block_edge
            ctx_at = contexts_of[slot_index] * block_edge
            user_rows = lax.dynamic_slice_in_dim(group_users, row_at, block_edge, 0)
            item_rows = lax.dynamic_slice_in_dim(all_items, item_at, block_edge, 0)
            context_rows = lax.dynamic_slice_in_dim(context_bf, ctx_at, block_edge, 0)
            user_term, item_term, context_term = block_terms(
                block_x, user_rows, item_rows, context_rows, is_last
            )
            user_acc = add_rows(user_acc, row_at, user_term)
            item_acc = add_rows(item_acc, item_at, item_term)
            item_tiles = lax.dynamic_update_index_in_dim(item_tiles, item_term, slot_index, 0)
            if is_last:
                ctx_acc = add_rows(ctx_acc, ctx_at, context_term)
            return (user_acc, item_acc, ctx_acc, item_tiles)

        start_acc = (
            jnp.zeros((row_groups * block_edge, factor_rank), jnp.float32),
            jnp.zeros((blk_count * block_edge, factor_rank), jnp.float32),
            jnp.zeros(context_factor.shape, jnp.float32),
            jnp.zeros((slot_count, block_edge, factor_rank), jnp.float32),
        )
        user_acc, item_acc, ctx_acc, item_tiles = lax.fori_loop(
            0, live_count, visit_block, start_acc
        )
        own_grad = lax.psum_scatter(user_acc, "rows", scatter_dimension=0, tiled=True)
        received = lax.all_to_all(
            item_acc.reshape(blk_count, block_edge, factor_rank),
            "blk",
            split_axis=0,
            concat_axis=0,
            tiled=True,
        )
        item_grad = lax.psum(jnp.sum(received, axis=0), "rows")
        user_factor = user_factor - user_step * own_grad
        item_factor = item_factor - item_step * item_grad
        if is_last:
            context_grad = lax.psum(ctx_acc, ("blk", "rows")) * grad_scale
    return (user_factor, item_factor, context_grad)


def solution(mesh):
    return jax.shard_map(
        local,
        mesh=mesh,
        in_specs=(
            P("blk", "rows", None, None, None),
            P("blk", "rows", None),
            P("blk", "rows", None),
            P("blk", "rows", None),
            P("blk", "rows"),
            P(("blk", "rows"), None),
            P("blk", None),
            P(),
        ),
        out_specs=(P(("blk", "rows"), None), P("blk", None), P()),
        check_vma=False,
    )
```

profile of v0, /device:TPU:1, one launch (start us, length us, event | category | flops | bytes accessed | tf_op | source)
XLA Modules:
  0.0 1447.4 jit_solution(12432927686246199933)
XLA Ops:
  7.2 1.5 convert_element_type.100
  8.7 0.8 convert_element_type.99
  9.6 0.9 convert_element_type.101
  10.5 29.7 %all_gather.12 = bf16[512,256]{1,0:T(8,128)(2,1)S(1)} all-gather(bf16[64,256]{1,0:T(8,128)(2,1)S(1)} %convert_element_type.99), channel_id=1, replica_groups=mesh['blk'=64,'rows'=8] {'rows'}, dimensions={0}, use_global_device_ids=true | all-gather | bytes 294912 | tf_op jit(solution)/shard_map/all_gather | solution.py:80
  40.2 98.4 %all-gather.3.cloned.1.call-done = bf16[4096,256]{1,0:T(8,128)(2,1)} async-done(((bf16[64,256]{1,0:T(8,128)(2,1)}), bf16[4096,256]{1,0:T(8,128)(2,1)}) %all-gather.3.cloned.1.call-update) | async-done | bytes 2097168 | tf_op jit(solution)/shard_map/all_gather | solution.py:81
  138.6 2.2 broadcast.33.clone
  140.9 12.0 while.30
  141.5 0.6 dynamic_slice.119
  142.8 0.6 dynamic_slice.121
  144.0 0.6 dynamic_slice.120
  145.3 0.8 dynamic-slice_convert_fusion.10
  146.1 0.7 multiply_convert_fusion.24
  146.8 1.8 fusion.57
  149.1 1.1 reshape.90
  150.2 2.0 fusion.59
  152.9 219.8 %all_to_all.10 = f32[64,64,256]{2,1,0:T(8,128)} all-to-all(f32[64,64,256]{2,1,0:T(8,128)} %bitcast.101), channel_id=1, replica_groups=mesh['blk'=64,'rows'=8] {'blk'}, dimensions={0} | all-to-all | bytes 8388608 | tf_op jit(solution)/shard_map/all_to_all | solution.py:112
  372.7 3.1 reduce_sum.18
  375.8 0.7 reduce-scatter.3.cloned.1.call-update
  376.6 86.1 %all-reduce.4.cloned.1.call-done = f32[64,256]{1,0:T(8,128)} async-done(((f32[64,256]{1,0:T(8,128)}), f32[64,256]{1,0:T(8,128)}) %all-reduce.4.cloned.1.call-update) | async-done | bytes 65552 | tf_op jit(solution)/shard_map/psum | solution.py:119
  462.6 1.5 fusion.24
  464.1 91.3 %reduce-scatter.3.cloned.1.call-done = f32[64,256]{1,0:T(8,128)} async-done(((f32[512,256]{1,0:T(8,128)}), f32[64,256]{1,0:T(8,128)}) %reduce-scatter.3.cloned.1.call-update) | async-done | bytes 65552 | tf_op jit(solution)/shard_map/reduce_scatter | solution.py:111
  555.5 0.9 fusion.23
  556.3 30.4 %all_gather.14 = bf16[512,256]{1,0:T(8,128)(2,1)} all-gather(bf16[64,256]{1,0:T(8,128)(2,1)S(1)} %fusion.23), channel_id=1, replica_groups=mesh['blk'=64,'rows'=8] {'rows'}, dimensions={0}, use_global_device_ids=true | all-gather | bytes 294912 | tf_op jit(solution)/shard_map/all_gather | solution.py:80
  586.7 94.9 %all-gather.5.cloned.1.call-done = bf16[4096,256]{1,0:T(8,128)(2,1)} async-done(((bf16[64,256]{1,0:T(8,128)(2,1)}), bf16[4096,256]{1,0:T(8,128)(2,1)}) %all-gather.5.cloned.1.call-update) | async-done | bytes 2097168 | tf_op jit(solution)/shard_map/all_gather | solution.py:81
  681.7 2.3 broadcast.33
  683.9 17.4 %while.31 = (s32[]{:T(128)}, f32[512,256]{1,0:T(8,128)S(1)}, f32[4096,256]{1,0:T(8,128)}, f32[128,256]{1,0:T(8,128)S(1)}, s32[]{:T(128)}, /*index=5*/s32[3]{0:T(...) while((s32[]{:T(128)}, f32[512,256]{1,0:T(8,128)S(1)}, ...), condition=%wide.region_6.7_spmd, body=%wide.region_5.6_spmd.sunk | while | flops 544047104 | bytes 16253349 | solution.py:108
  684.6 0.6 dynamic_slice.129
  685.9 0.6 dynamic_slice.131
  687.1 0.6 dynamic_slice.130
  688.3 0.8 dynamic-slice_convert_fusion.13
  689.1 0.8 dynamic-slice_convert_fusion.12
  689.9 1.5 multiply_convert_fusion.26
  691.4 1.8 fusion.67
  693.7 2.1 reshape.92
  695.8 1.8 fusion.70
  697.5 1.1 reshape.91
  698.7 2.0 fusion.69
  701.4 0.8 copy-done
  702.2 42.3 %all-to-all-start.1 = ((f32[64,64,256]{2,1,0:T(8,128)}), f32[64,64,256]{2,1,0:T(8,128)}, u32[]{:S(2)}, u32[]{:S(2)}) async-start(f32[64,64,256]{2,1,0:T(8,128)} %bitcast.100), calls=%async_computation.3 | async-start | bytes 8388608 | tf_op jit(solution)/shard_map/all_to_all | solution.py:112
  744.6 0.5 all-reduce.8.cloned.1.call-update
  745.2 0.5 reduce-scatter.5.cloned.1.call-update
  745.8 516.4 %all-reduce.8.cloned.1.call-done = f32[128,256]{1,0:T(8,128)} async-done(((f32[128,256]{1,0:T(8,128)}), f32[128,256]{1,0:T(8,128)}) %all-reduce.8.cloned.1.call-update) | async-done | bytes 131088 | tf_op jit(solution)/shard_map/psum | solution.py:123
  1262.1 1.6 broadcast_multiply_fusion
  1263.7 3.1 reduce_sum.19
  1266.8 74.4 %reduce-scatter.5.cloned.1.call-done = f32[64,256]{1,0:T(8,128)} async-done(((f32[512,256]{1,0:T(8,128)}), f32[64,256]{1,0:T(8,128)}) %reduce-scatter.5.cloned.1.call-update) | async-done | bytes 65552 | tf_op jit(solution)/shard_map/reduce_scatter | solution.py:111
  1341.2 1.5 multiply_subtract_fusion.1
  1342.7 96.3 %all-reduce.6.cloned.1.call-done = f32[64,256]{1,0:T(8,128)} async-done(((f32[64,256]{1,0:T(8,128)}), f32[64,256]{1,0:T(8,128)}) %all-reduce.6.cloned.1.call-update) | async-done | bytes 65552 | tf_op jit(solution)/shard_map/psum | solution.py:119
  1439.1 1.5 multiply_subtract_fusion
  (39 shorter events, 1.4 us)
Async XLA Ops:
  7.2 131.4 %all-gather.3.cloned.1.call-start = ((), (), s32[]{:S(2)}) async-start(), calls=%async_computation.4 | async-start | bytes 2129920 | tf_op jit(solution)/shard_map/all_gather | solution.py:81
  8.7 453.9 %all-reduce.4.cloned.1.call-start = ((), (), s32[]{:S(2)}) async-start(), calls=%async_computation.6 | async-start | bytes 131072 | tf_op jit(solution)/shard_map/psum | solution.py:119
  138.6 2.3 copy-start.8
  138.6 2.3 copy-start.9
  138.6 2.3 copy-start.10
  152.9 219.8 %copy-start.1 = (f32[512,256]{1,0:T(8,128)}, f32[512,256]{1,0:T(8,128)S(1)}, u32[]{:S(2)}) copy-start(f32[512,256]{1,0:T(8,128)S(1)} %get-tuple-element.185) | copy-start | bytes 1572868
  372.7 90.0 %copy-start.4 = (f32[64,256]{1,0:T(8,128)S(1)}, f32[64,256]{1,0:T(8,128)}, u32[]{:S(2)}) copy-start(f32[64,256]{1,0:T(8,128)} %param.18) | copy-start | bytes 196612
  372.7 182.8 %copy-start.3 = (f32[64,256]{1,0:T(8,128)S(1)}, f32[64,256]{1,0:T(8,128)}, u32[]{:S(2)}) copy-start(f32[64,256]{1,0:T(8,128)} %param.17) | copy-start | bytes 196612
  375.8 179.7 %reduce-scatter.3.cloned.1.call-start = ((), (), s32[]{:S(2)}) async-start(), calls=%async_computation.5 | async-start | bytes 589824 | tf_op jit(solution)/shard_map/reduce_scatter | solution.py:111
  376.5 305.1 %all-gather.5.cloned.1.call-start = ((), (), s32[]{:S(2)}) async-start(), calls=%async_computation.7 | async-start | bytes 2129920 | tf_op jit(solution)/shard_map/all_gather | solution.py:81
  701.3 0.8 copy-start
  701.4 0.8 copy-start.2
  702.2 561.5 %all-to-all-start.1 = ((f32[64,64,256]{2,1,0:T(8,128)}), f32[64,64,256]{2,1,0:T(8,128)}, u32[]{:S(2)}, u32[]{:S(2)}) async-start(f32[64,64,256]{2,1,0:T(8,128)} %bitcast.100), calls=%async_computation.3 | async-start | bytes 8388608 | tf_op jit(solution)/shard_map/all_to_all | solution.py:112
  744.5 517.6 %all-reduce.8.cloned.1.call-start = ((), (), s32[]{:S(2)}) async-start(), calls=%async_computation.10 | async-start | bytes 262144 | tf_op jit(solution)/shard_map/psum | solution.py:123
  745.1 596.1 %reduce-scatter.5.cloned.1.call-start = ((), (), s32[]{:S(2)}) async-start(), calls=%async_computation.8 | async-start | bytes 589824 | tf_op jit(solution)/shard_map/reduce_scatter | solution.py:111
  745.7 693.3 %all-reduce.6.cloned.1.call-start = ((), (), s32[]{:S(2)}) async-start(), calls=%async_computation.9 | async-start | bytes 131072 | tf_op jit(solution)/shard_map/psum | solution.py:119
  1263.7 77.6 %copy-start.7 = (f32[64,256]{1,0:T(8,128)S(1)}, f32[64,256]{1,0:T(8,128)}, u32[]{:S(2)}) copy-start(f32[64,256]{1,0:T(8,128)} %reduce-scatter.3.cloned.1.call-done) | copy-start | bytes 196612
  1263.7 175.4 %copy-start.5 = (f32[64,256]{1,0:T(8,128)S(1)}, f32[64,256]{1,0:T(8,128)}, u32[]{:S(2)}) copy-start(f32[64,256]{1,0:T(8,128)} %param.18) | copy-start | bytes 196612
  1263.7 175.4 %copy-start.6 = (f32[64,256]{1,0:T(8,128)S(1)}, f32[64,256]{1,0:T(8,128)}, u32[]{:S(2)}) copy-start(f32[64,256]{1,0:T(8,128)} %all-reduce.4.cloned.1.call-done) | copy-start | bytes 196612
Sparse Core Ops, SparseCore 0:
  10.7 127.7 all-gather.2
  375.9 86.6 all-reduce.3
  467.7 87.6 reduce-scatter.2
  558.0 123.5 all-gather.4
  751.1 510.9 all-reduce.7
  1267.1 74.1 reduce-scatter.4
  1344.7 94.2 all-reduce.5
where the time goes:
time: 1450 us
  waiting for transfers between devices  1060 us (73%)
  blocking collectives  280 us (19%)
  starting transfers between devices  42.6 us (3%)
  other arithmetic  20.8 us (1%)
    psum x1, waiting for transfers between devices, local(): context_grad = lax.psum(ctx_acc, ('blk', 'rows')) * grad_scale  516 us
    all_to_all x1, blocking collectives, local(): lax.all_to_all(item_acc.reshape(blk_count, block_edge, factor_rank), 'blk...  220 us
    all_gather x2, waiting for transfers between devices, local(): lax.all_gather(item_factor.astype(jnp.bfloat16), 'blk', axis=0, tiled=True)  193 us
    psum x2, waiting for transfers between devices, local(): item_grad = lax.psum(jnp.sum(received, axis=0), 'rows')  182 us
    reduce_scatter x2, waiting for transfers between devices, local(): lax.psum_scatter(user_acc, 'rows', scatter_dimension=0, tiled=True)  166 us
    all_gather x2, blocking collectives, local(): lax.all_gather(user_factor.astype(jnp.bfloat16), 'rows', axis=0, tiled=True)  60.1 us
    all_to_all x1, starting transfers between devices, local(): lax.all_to_all(item_acc.reshape(blk_count, block_edge, factor_rank), 'blk...  42.3 us
  transfers between devices with their start and end apart: 8, of which 7 were waited for; matrix products, arithmetic and copies ran while one was open for 1% of the time, Pallas kernels for 0%

commit v1 on v0

v1 whole, which is shorter than its diff:
```python
import functools
import math

import jax
import jax.numpy as jnp
from jax import lax
from jax.experimental import pallas as pl
from jax.experimental.pallas import tpu as pltpu
from jax.sharding import PartitionSpec as P

ITERS = 2
NQ = 4
MESH = pl.DeviceIdType.MESH
F32 = jnp.float32
BF16 = jnp.bfloat16


def stack_halves(x):
    return jnp.concatenate([x[..., :128], x[..., 128:]], axis=-2)


def unstack_halves(x):
    n = x.shape[-2] // 2
    return jnp.concatenate([x[..., :n, :], x[..., n:, :]], axis=-1)


class Exchange:
    def __init__(self, n, me, dev, src, land, send, recv):
        self.n, self.me, self.dev, self.src, self.land = n, me, dev, src, land
        self.send, self.recv = send, recv

    def _copy(self, step):
        to = lax.rem(self.me + step, self.n)
        return pltpu.make_async_remote_copy(
            src_ref=self.src(to),
            dst_ref=self.land(self.me),
            send_sem=self.send.at[step - 1],
            recv_sem=self.recv.at[step - 1],
            device_id=self.dev(to),
            device_id_type=MESH,
        )

    def _arrival(self, step):
        frm = lax.rem(self.me + self.n - step, self.n)
        return pltpu.make_async_remote_copy(
            src_ref=self.land(frm),
            dst_ref=self.land(frm),
            send_sem=self.send.at[step - 1],
            recv_sem=self.recv.at[step - 1],
            device_id=self.dev(frm),
            device_id_type=MESH,
        )

    def start(self):
        @pl.loop(1, self.n)
        def _(step):
            self._copy(step).start()

    def wait(self):
        @pl.loop(1, self.n)
        def _(step):
            self._arrival(step).wait_recv()

    def finish(self):
        @pl.loop(1, self.n)
        def _(step):
            self._copy(step).wait_send()


def kernel(
    nz, nr, user_step, item_step, grad_scale,
    blocks, row_of, col_of, ctx_of, live_of, user_in, item_in, ctx_in,
    new_users, new_items, ctx_out,
    xb, gu, idx, bmat, amat, zg, qg, ys, rg, vf, wf, ub, user_t, item_t, ctx_t,
    xs0, xr0, xs1, xr1, us, ur, qs, qr, zs, zr, cqs, cqr, cz, cq2, fin,
    xsem, rsend, rrecv, qsend, qrecv, zsend, zrecv,
):
    blk = lax.axis_index("blk")
    r = lax.axis_index("rows")
    z, q = blk // NQ, lax.rem(blk, NQ)
    slots = xb.shape[0]
    nb = nz * NQ

    def row_dev(i):
        return (blk, i)

    def q_dev(i):
        return (z * NQ + i, r)

    def z_dev(i):
        return (i * NQ + q, r)

    pending = []
    used = {"r": 0, "q": 0, "z": 0}

    def exchange(kind, src, land):
        n, me, dev, send, recv = {
            "r": (nr, r, row_dev, rsend, rrecv),
            "q": (NQ, q, q_dev, qsend, qrecv),
            "z": (nz, z, z_dev, zsend, zrecv),
        }[kind]
        at = used[kind]
        used[kind] += 1
        e = Exchange(n, me, dev, src, land, send.at[at], recv.at[at])
        e.start()
        pending.append(e)
        return e

    load = pltpu.make_async_copy(blocks.at[0, 0], xb, xsem)
    load.start()

    barrier = pltpu.get_barrier_semaphore()
    for n, me, dev in ((nr, r, row_dev), (NQ, q, q_dev), (nz, z, z_dev)):

        @pl.loop(1, n)
        def _(step):
            pl.semaphore_signal(
                barrier, inc=1, device_id=dev(lax.rem(me + step, n)), device_id_type=MESH
            )

    live = live_of[0, 0]
    rows = [row_of[0, 0, s] for s in range(slots)]
    ctxs = [ctx_of[0, 0, s] for s in range(slots)]
    alive = [(s < live).astype(jnp.int32) for s in range(slots)]

    i16 = lax.broadcasted_iota(jnp.int32, (16, 128), 0)
    for s in range(slots):
        col = col_of[0, 0, s]
        place = ((col & (NQ - 1)) * nz + (col >> 2)) * 16
        target = (i16 + place) * alive[s] + (alive[s] - 1)
        idx[r, pl.ds(16 * s, 16), :] = target

    user_own = user_in[...]
    item_own = stack_halves(item_in[pl.ds(pl.multiple_of(r * 8, 8), 8), :])
    gu[0, r] = user_own.astype(BF16)
    zg[0, z] = item_own.astype(BF16)
    for s in range(slots):
        w = ctx_in[...].astype(BF16).astype(F32)
        second = ctxs[s].astype(F32)
        wf[s] = w[:64] * (1.0 - second) + w[64:] * second

    pl.semaphore_wait(barrier, nr - 1 + NQ - 1 + nz - 1)

    for k in range(ITERS):
        last = k == ITERS - 1
        z_gather = exchange("z", lambda i, k=k: zg.at[k, z], lambda i, k=k: zg.at[k, i])
        if k == 0:
            index_gather = exchange("r", lambda i: idx.at[r], lambda i: idx.at[i])
            user_gather = exchange("r", lambda i: gu.at[0, r], lambda i: gu.at[0, i])
        z_gather.wait()
        qg[k, q] = zg[k]
        q_gather = exchange("q", lambda i, k=k: zg.at[k], lambda i, k=k: qg.at[k, i])
        if k == 0:
            index_gather.wait()
            wanted = idx[...].reshape(nr * slots * 16, 128)
            count = nr * slots * 16
            lane = lax.broadcasted_iota(jnp.int32, (count, 128), 1)
            for c in range(nb * 16 // 128):
                hit = jnp.where(lane + 128 * c == wanted, 1.0, 0.0)
                bmat[:, 128 * c : 128 * (c + 1)] = hit.astype(BF16)
            row16 = lax.broadcasted_iota(jnp.int32, (nb * 16, 128), 0)
            i0 = lax.broadcasted_iota(jnp.int32, (128, 128), 0)
            i1 = lax.broadcasted_iota(jnp.int32, (128, 128), 1)
            for c in range(count // 128):
                part = jnp.where(i0 == i1, wanted[128 * c : 128 * (c + 1)], 0)
                along = jnp.sum(part, axis=0, keepdims=True)
                hit = jnp.where(row16 == along, 1.0, 0.0)
                amat[:, 128 * c : 128 * (c + 1)] = hit.astype(BF16)
        q_gather.wait()
        shares = qg[k].reshape(nb * 16, 128)
        picked = jnp.dot(bmat[...], shares, preferred_element_type=F32)
        ys[k] = picked.astype(BF16).reshape(nr, slots * 16, 128)
        rg[k, r] = ys[k, r]
        item_answer = exchange("r", lambda i, k=k: ys.at[k, i], lambda i, k=k: rg.at[k, i])
        user_gather.wait()
        for s in range(slots):
            total = jnp.zeros((64, 256), F32)
            for p in range(nr):
                total += gu[k, p].astype(F32) * (rows[s] == p).astype(jnp.int32).astype(F32)
            ub[s] = total.astype(BF16)
        item_answer.wait()
        for s in range(slots):
            part = rg[k, :, pl.ds(16 * s, 16), :].astype(F32)
            vf[s] = unstack_halves(part).reshape(64, 256)
        if k == 0:
            load.wait()
        user_t[...] = jnp.zeros_like(user_t)
        if last:
            ctx_t[...] = jnp.zeros_like(ctx_t)

        @pl.loop(0, 8)
        def _(c):
            for s in range(slots):
                u, w = ub[s], wf[s]
                v = vf[s, pl.ds(pl.multiple_of(c * 8, 8), 8), :]
                pair = (v[:, None, :] * w[None, :, :]).astype(BF16).reshape(512, 256)
                model = lax.dot_general(
                    u, pair, (((1,), (1,)), ((), ())), preferred_element_type=F32
                )
                x = xb[s, :, pl.ds(pl.multiple_of(c * 512, 512), 512)]
                resid = (model - x.astype(F32)).astype(BF16)
                user_t[s] += jnp.dot(resid, pair, preferred_element_type=F32)
                g = lax.dot_general(
                    resid, u, (((0,), (0,)), ((), ())), preferred_element_type=F32
                ).reshape(8, 64, 256)
                item_t[s, pl.ds(pl.multiple_of(c * 8, 8), 8), :] = jnp.sum(g * w[None], axis=1)
                if last:
                    ctx_t[s] += jnp.sum(g * v[:, None, :], axis=0)

        xs, xr = (xs1, xr1) if last else (xs0, xr0)
        for s in range(slots):
            tile = item_t[s].reshape(nr, 8, 256)
            xs[:, pl.ds(16 * s, 16), :] = stack_halves(tile).astype(BF16)
        if last:
            for c in range(2):
                total = jnp.zeros((64, 256), F32)
                for s in range(slots):
                    mine = alive[s] * (ctxs[s] == c).astype(jnp.int32)
                    total += ctx_t[s] * mine.astype(F32)
                tile = stack_halves(total.reshape(nr, 8, 256))
                xs[:, pl.ds(16 * (slots + c), 16), :] = tile.astype(BF16)
        xr[r] = xs[r]
        item_parts = exchange("r", lambda i, xs=xs: xs.at[i], lambda i, xr=xr: xr.at[i])
        for p in range(nr):
            total = jnp.zeros((64, 256), F32)
            for s in range(slots):
                mine = alive[s] * (rows[s] == p).astype(jnp.int32)
                total += user_t[s] * mine.astype(F32)
            us[k, p] = total.astype(BF16)
        ur[k, r] = us[k, r]
        user_parts = exchange("r", lambda i, k=k: us.at[k, i], lambda i, k=k: ur.at[k, i])

        item_parts.wait()
        parts = xr[:, : slots * 16, :].reshape(nr * slots * 16, 128)
        summed = jnp.dot(amat[...], parts, preferred_element_type=F32)
        qs[k] = summed.astype(BF16).reshape(NQ, nz, 16, 128)
        qr[k, q] = qs[k, q]
        q_parts = exchange("q", lambda i, k=k: qs.at[k, i], lambda i, k=k: qr.at[k, i])
        if last:
            total = jnp.sum(xr[:, slots * 16 :, :].astype(F32), axis=0)
            cqs[...] = total.reshape(NQ, 8, 128)
            cqr[q] = cqs[q]
            ctx_q = exchange("q", lambda i: cqs.at[i], lambda i: cqr.at[i])
        user_parts.wait()
        user_own = user_own - user_step * jnp.sum(ur[k].astype(F32), axis=0)
        if last:
            new_users[...] = user_own
        else:
            gu[k + 1, r] = user_own.astype(BF16)
            user_gather = exchange(
                "r", lambda i, k=k: gu.at[k + 1, r], lambda i, k=k: gu.at[k + 1, i]
            )
        q_parts.wait()
        zs[k] = jnp.sum(qr[k].astype(F32), axis=0).astype(BF16)
        zr[k, z] = zs[k, z]
        z_parts = exchange("z", lambda i, k=k: zs.at[k, i], lambda i, k=k: zr.at[k, i])
        if last:
            ctx_q.wait()
            cz[z] = jnp.sum(cqr[...], axis=0)
            ctx_z = exchange("z", lambda i: cz.at[z], lambda i: cz.at[i])
        z_parts.wait()
        item_own = item_own - item_step * jnp.sum(zr[k].astype(F32), axis=0)
        if not last:
            zg[k + 1, z] = item_own.astype(BF16)

    ctx_z.wait()
    cq2[q] = jnp.sum(cz[...], axis=0) * grad_scale
    ctx_gather = exchange("q", lambda i: cq2.at[q], lambda i: cq2.at[i])
    ctx_gather.wait()
    fin[r, pl.ds(0, 16), :] = item_own
    fin[r, pl.ds(16, 32), :] = cq2[...].reshape(32, 128)
    last_gather = exchange("r", lambda i: fin.at[r], lambda i: fin.at[i])
    last_gather.wait()
    new_items[...] = unstack_halves(fin[:, :16, :]).reshape(64, 256)
    for c in range(2):
        part = fin[:, pl.ds(16 + 16 * c, 16), :]
        ctx_out[pl.ds(64 * c, 64), :] = unstack_halves(part).reshape(64, 256)
    for e in pending:
        e.finish()


def local(
    blocks, block_row, block_col, block_ctx, live_blocks, user_factor, item_factor, context_factor
):
    nr = lax.axis_size("rows")
    nz = lax.axis_size("blk") // NQ
    slots = blocks.shape[2]
    nb = nz * NQ
    edge = blocks.shape[3]
    vm = pltpu.VMEM
    dma = pltpu.SemaphoreType.DMA
    scratch = [
        vm((slots, 64, 4096), BF16),
        vm((ITERS, nr, 64, 256), BF16),
        vm((nr, slots * 16, 128), jnp.int32),
        vm((nr * slots * 16, nb * 16), BF16),
        vm((nb * 16, nr * slots * 16), BF16),
        vm((ITERS, nz, 16, 128), BF16),
        vm((ITERS, NQ, nz, 16, 128), BF16),
        vm((ITERS, nr, slots * 16, 128), BF16),
        vm((ITERS, nr, slots * 16, 128), BF16),
        vm((slots, 64, 256), F32),
        vm((slots, 64, 256), F32),
        vm((slots, 64, 256), BF16),
        vm((slots, 64, 256), F32),
        vm((slots, 64, 256), F32),
        vm((slots, 64, 256), F32),
        vm((nr, slots * 16, 128), BF16),
        vm((nr, slots * 16, 128), BF16),
        vm((nr, slots * 16 + 32, 128), BF16),
        vm((nr, slots * 16 + 32, 128), BF16),
        vm((ITERS, nr, 64, 256), BF16),
        vm((ITERS, nr, 64, 256), BF16),
        vm((ITERS, NQ, nz, 16, 128), BF16),
        vm((ITERS, NQ, nz, 16, 128), BF16),
        vm((ITERS, nz, 16, 128), BF16),
        vm((ITERS, nz, 16, 128), BF16),
        vm((NQ, 8, 128), F32),
        vm((NQ, 8, 128), F32),
        vm((nz, 8, 128), F32),
        vm((NQ, 8, 128), F32),
        vm((nr, 48, 128), F32),
        dma,
        dma((10, nr - 1)),
        dma((10, nr - 1)),
        dma((6, NQ - 1)),
        dma((6, NQ - 1)),
        dma((5, nz - 1)),
        dma((5, nz - 1)),
    ]
    body = functools.partial(
        kernel,
        nz,
        nr,
        6.4 / (edge * edge),
        16.0 / (edge * edge * nr),
        8.0 / (edge * math.sqrt(nb * nr)),
    )
    in_vmem = pl.BlockSpec(memory_space=pltpu.VMEM)
    in_smem = pl.BlockSpec(memory_space=pltpu.SMEM)
    return pl.pallas_call(
        body,
        out_shape=(
            jax.ShapeDtypeStruct(user_factor.shape, F32),
            jax.ShapeDtypeStruct(item_factor.shape, F32),
            jax.ShapeDtypeStruct(context_factor.shape, F32),
        ),
        in_specs=[pl.BlockSpec(memory_space=pl.ANY)] + [in_smem] * 4 + [in_vmem] * 3,
        out_specs=(in_vmem,) * 3,
        scratch_shapes=scratch,
        compiler_params=pltpu.CompilerParams(
            collective_id=0, has_side_effects=True, vmem_limit_bytes=40 * 1024 * 1024
        ),
    )(
        blocks, block_row, block_col, block_ctx, live_blocks,
        user_factor, item_factor, context_factor,
    )


def solution(mesh):
    return jax.shard_map(
        local,
        mesh=mesh,
        in_specs=(
            P("blk", "rows", None, None, None),
            P("blk", "rows", None),
            P("blk", "rows", None),
            P("blk", "rows", None),
            P("blk", "rows"),
            P(("blk", "rows"), None),
            P("blk", None),
            P(),
        ),
        out_specs=(P(("blk", "rows"), None), P("blk", None), P()),
        check_vma=False,
    )
```

time: 1450 us -> 135 us (0.09)
  waiting for transfers between devices: 1060 us -> 0 us
  blocking collectives: 280 us -> 0 us
  Pallas kernels: 0 us -> 126 us
  starting transfers between devices: 42.6 us -> 0 us
  other arithmetic: 20.8 us -> 0 us
    psum x3 -> x0, waiting for transfers between devices: 699 us -> none  [the longest x1 516 us: local(): context_grad = lax.psum(ctx_acc, ('blk', 'rows')) * grad_scale]
    all_to_all x1 -> x0, blocking collectives: 220 us -> none  [local(): lax.all_to_all(item_acc.reshape(blk_count, block_edge, factor_rank), 'blk...]
    all_gather x2 -> x0, waiting for transfers between devices: 193 us -> none  [local(): lax.all_gather(item_factor.astype(jnp.bfloat16), 'blk', axis=0, tiled=True)]
    reduce_scatter x2 -> x0, waiting for transfers between devices: 166 us -> none  [local(): lax.psum_scatter(user_acc, 'rows', scatter_dimension=0, tiled=True)]
    pallas_call x0 -> x1, Pallas kernels: none -> 126 us  [local(): pl.pallas_call(body, out_shape=(jax.ShapeDtypeStruct(user_factor.shape, F...]
    all_gather x2 -> x0, blocking collectives: 60.1 us -> none  [local(): lax.all_gather(user_factor.astype(jnp.bfloat16), 'rows', axis=0, tiled=True)]
    all_to_all x1 -> x0, starting transfers between devices: 42.3 us -> none  [local(): lax.all_to_all(item_acc.reshape(blk_count, block_edge, factor_rank), 'blk...]
  transfers between devices with their start and end apart: 8 -> 0, of which waited for: 7 -> 0; matrix products, arithmetic and copies ran while one was open for 1% -> 0% of each run, Pallas kernels for 0% -> 0%
where the time goes in v1:
time: 135 us
  Pallas kernels  126 us (93%)
  local copies, waits for them, and re-layouts  7.86 us (6%)
    pallas_call x1, Pallas kernels, local(): pl.pallas_call(body, out_shape=(jax.ShapeDtypeStruct(user_factor.shape, F...  126 us
    unnamed x17, local copies, waits for them, and re-layouts  7.86 us

profile of v1, /device:TPU:1, one launch (start us, length us, event | category | flops | bytes accessed | tf_op | source)
XLA Modules:
  0.0 135.1 jit_solution(17356722693026135169)
XLA Ops:
  1.3 0.0 copy-start
  1.3 1.4 %copy-done = bf16[1,1,3,64,4096]{4,3,2,1,0:T(8,128)(2,1)S(1)} copy-done((bf16[1,1,3,64,4096]{4,3,2,1,0:T(8,128)(2,1)S(1)}, bf16[1,1,3,64,4096]{4,3,2,1,0:T(8,128)(2,1)}, u32[]{:S(2)}) %copy-start) | copy-done | bytes 1572888
  2.7 0.0 copy-start.1
  2.7 0.9 copy-done.1
  3.6 0.0 copy-start.2
  3.6 0.8 copy-done.2
  4.4 0.0 copy-start.3
  4.4 0.8 copy-done.3
  5.3 0.0 copy-start.4
  5.3 0.7 copy-done.4
  5.9 0.0 copy-start.5
  5.9 0.7 copy-done.5
  6.6 0.0 copy-start.6
  6.6 0.7 copy-done.6
  7.2 126.0 %shard_map.103 = (f32[64,256]{1,0:T(8,128)S(1)}, f32[64,256]{1,0:T(8,128)S(1)}, f32[128,256]{1,0:T(8,128)S(1)}) custom-call(bf16[1,1,3,64,4096]{4,3,2,1,0:T(8,128)(2,1)S(1)} %copy-done, s32[1,1,3]{2,1,0:T(1,128)S(1)} %copy-done.4, s32[1,1,3]{2,1,0:T(1,128)S(1)} %copy-done.5, s32[1,1,3]{2,1,0:T(1,128)S(1)} %copy-done.6, s32[1,1]{1,0:T(1,128)S(6)} %copy.14.live_of, ...), custom_call_target="tpu_custom_call" | custom-call | tf_op jit(solution)/shard_map/pallas_call | solution.py:341
  133.2 0.6 copy.15
  133.8 0.6 copy.16
  134.5 0.7 copy.17
Async XLA Ops:
  1.3 1.4 %copy-start = (bf16[1,1,3,64,4096]{4,3,2,1,0:T(8,128)(2,1)S(1)}, bf16[1,1,3,64,4096]{4,3,2,1,0:T(8,128)(2,1)}, u32[]{:S(2)}) copy-start(bf16[1,1,3,64,4096]{4,3,2,1,0:T(8,128)(2,1)} %blocks.1) | copy-start | bytes 4718596
  2.7 0.9 copy-start.1
  3.6 0.8 copy-start.2
  4.4 0.8 copy-start.3
  5.3 0.7 copy-start.4
  5.9 0.7 copy-start.5
  6.6 0.7 copy-start.6

commit v2 on v1

v2 whole, which is shorter than its diff:
```python
import functools
import math

import jax
import jax.numpy as jnp
from jax import lax
from jax.experimental import pallas as pl
from jax.experimental.pallas import tpu as pltpu
from jax.sharding import PartitionSpec as P

ITERS = 2
NQ = 4
MESH = pl.DeviceIdType.MESH
F32 = jnp.float32
BF16 = jnp.bfloat16


class Exchange:
    def __init__(self, group, src, land, send, recv):
        self.steps, self.me, self.peer, self.source, self.dev = group
        self.src, self.land, self.send, self.recv = src, land, send, recv

    def _copy(self, i):
        to = self.peer(i)
        return pltpu.make_async_remote_copy(
            src_ref=self.src(to),
            dst_ref=self.land(self.me),
            send_sem=self.send.at[i],
            recv_sem=self.recv.at[i],
            device_id=self.dev(to),
            device_id_type=MESH,
        )

    def _arrival(self, i):
        frm = self.source(i)
        return pltpu.make_async_remote_copy(
            src_ref=self.land(frm),
            dst_ref=self.land(frm),
            send_sem=self.send.at[i],
            recv_sem=self.recv.at[i],
            device_id=self.dev(frm),
            device_id_type=MESH,
        )

    def start(self):
        @pl.loop(0, self.steps)
        def _(i):
            self._copy(i).start()

    def wait(self):
        @pl.loop(0, self.steps)
        def _(i):
            self._arrival(i).wait_recv()

    def finish(self):
        @pl.loop(0, self.steps)
        def _(i):
            self._copy(i).wait_send()


def ring(n, me, dev, far_first):
    def offset(i):
        if not far_first:
            return i + 1
        return n // 2 + (1 - 2 * (i % 2)) * ((i + 1) // 2)

    return (
        n - 1,
        me,
        lambda i: lax.rem(me + offset(i), n),
        lambda i: lax.rem(me + n - offset(i), n),
        dev,
    )


def plane(nr, q, r, dev):
    y_lo, core, y_hi, x = q // 2, lax.rem(q, 2), r // 4, lax.rem(r, 4)
    n = NQ * nr

    def member(i, sign):
        t = n - 1 - i
        b = (t // 4) % 4
        dx = (3 * b + 3 * (b // 2) - 2 * (b // 3)) % 4
        to_x = lax.rem(x + 4 + sign * dx, 4)
        to_hi = lax.rem(y_hi + t // 16, 2)
        to_lo = lax.rem(y_lo + (t // 2) % 2, 2)
        to_core = lax.rem(core + t % 2, 2)
        return (to_lo * 2 + to_core) * nr + to_hi * 4 + to_x

    return (n - 1, q * nr + r, lambda i: member(i, 1), lambda i: member(i, -1), dev)


def to_tiles(x):
    y = x.reshape(8, 8, 256)
    return jnp.stack([y[..., :128], y[..., 128:]], axis=1).reshape(16, 8, 128)


def from_tiles(x):
    y = x.reshape(8, 2, 8, 128)
    return jnp.concatenate([y[:, 0], y[:, 1]], axis=-1).reshape(64, 256)


def join_shares(x):
    y = x.reshape(16, 2, 4, 128)
    return from_tiles(jnp.concatenate([y[:, 0], y[:, 1]], axis=1))


def kernel(
    nz, nr, user_step, item_step, grad_scale,
    blocks, row_hbm, col_hbm, ctx_hbm, live_hbm, user_hbm, item_hbm, factor_hbm,
    new_users, new_items, ctx_out,
    xb, gu, idx, bmat, amat, iq, ist, zg, ys, rg, vf, wf, ub, user_t, item_t, ctx_t,
    xs0, xr0, xs1, xr1, us, ur, zs, zr, cz, fs, fin,
    row_of, col_of, ctx_of, live_of, user_in, item_in, ctx_in, insem,
    xsem, rsend, rrecv, qsend, qrecv, zsend, zrecv, psend, precv,
):
    blk = lax.axis_index("blk")
    r = lax.axis_index("rows")
    z, q = blk // NQ, lax.rem(blk, NQ)
    me = q * nr + r
    slots = xb.shape[0]
    members = NQ * nr
    groups = {
        "r": ring(nr, r, lambda i: (blk, i), False),
        "q": ring(NQ, q, lambda i: (z * NQ + i, r), False),
        "z": ring(nz, z, lambda i: (i * NQ + q, r), True),
        "p": plane(nr, q, r, lambda i: (z * NQ + i // nr, lax.rem(i, nr))),
    }
    semaphores = {
        "r": (rsend, rrecv), "q": (qsend, qrecv), "z": (zsend, zrecv), "p": (psend, precv),
    }

    pending = []
    used = {"r": 0, "q": 0, "z": 0, "p": 0}

    def exchange(kind, src, land):
        send, recv = semaphores[kind]
        at = used[kind]
        used[kind] += 1
        e = Exchange(groups[kind], src, land, send.at[at], recv.at[at])
        e.start()
        pending.append(e)
        return e

    barrier = pltpu.get_barrier_semaphore()
    for kind in ("z", "p"):
        steps, _, peer, _, dev = groups[kind]

        @pl.loop(0, steps)
        def _(i):
            pl.semaphore_signal(
                barrier, inc=1, device_id=dev(peer(i)), device_id_type=MESH
            )

    inputs = [
        pltpu.make_async_copy(src, dst, insem.at[i])
        for i, (src, dst) in enumerate(
            (
                (item_hbm, item_in),
                (live_hbm, live_of),
                (col_hbm, col_of),
                (user_hbm, user_in),
                (row_hbm, row_of),
                (ctx_hbm, ctx_of),
                (factor_hbm, ctx_in),
            )
        )
    ]
    for c in inputs:
        c.start()
    load = pltpu.make_async_copy(blocks.at[0, 0], xb, xsem)
    load.start()
    for c in inputs:
        c.wait()
    live = live_of[0, 0]
    rows = [row_of[0, 0, s] for s in range(slots)]
    ctxs = [ctx_of[0, 0, s] for s in range(slots)]
    alive = [(s < live).astype(jnp.int32) for s in range(slots)]

    item_tiles = to_tiles(item_in[...])
    halves = [item_tiles, jnp.concatenate([item_tiles[:, 4:], item_tiles[:, :4]], axis=1)]
    ist[...] = jnp.stack(halves, axis=1).reshape(members, 8, 128)
    iq[q] = ist[me]
    sub = lax.broadcasted_iota(jnp.int32, (8, 128), 0)
    start = jnp.full((8, 128), -1000, jnp.int32)
    for s in range(slots):
        at = (col_of[0, 0, s] * 4) * alive[s] - 1000 * (1 - alive[s])
        start = jnp.where(sub == s, at, start)
    idx[me] = start
    user_own = user_in[...]
    gu[0, r] = user_own.astype(BF16)

    pl.semaphore_wait(barrier, nz - 1 + members - 1)

    item_first = exchange("q", lambda i: ist.at[i * nr + r], lambda i: iq.at[i])
    index_gather = exchange("p", lambda i: idx.at[me], lambda i: idx.at[i])
    item_first.wait()
    item_own = jnp.concatenate([iq[i][:4] for i in range(NQ)], axis=0)
    item_delta = jnp.zeros((16, 128), F32)
    zg[0, z] = item_own.astype(BF16)

    for k in range(ITERS):
        last = k == ITERS - 1
        z_gather = exchange("z", lambda i, k=k: zg.at[k, z], lambda i, k=k: zg.at[k, i])
        if k == 0:
            user_gather = exchange("r", lambda i: gu.at[0, r], lambda i: gu.at[0, i])
            for s in range(slots):
                w = ctx_in[...].astype(BF16).astype(F32)
                second = ctxs[s].astype(F32)
                wf[s] = w[:64] * (1.0 - second) + w[64:] * second
            index_gather.wait()
            sub3 = lax.broadcasted_iota(jnp.int32, (members, 8, 128), 1)
            row = [
                jnp.broadcast_to(idx[:, pl.ds(s, 1), :], (members, 8, 128)) for s in range(slots)
            ]
            first = jnp.where(sub3 < 4, row[0], row[1]) + lax.rem(sub3, 4)
            second = jnp.where(sub3 < 4, row[2], -1000) + lax.rem(sub3, 4)
            count = members * 16
            wanted = jnp.concatenate([first, second], axis=1).reshape(count, 128)
            total_rows = nz * 16
            lane = lax.broadcasted_iota(jnp.int32, (count, 128), 1)
            for c in range(total_rows // 128):
                hit = jnp.where(lane + 128 * c == wanted, 1.0, 0.0)
                bmat[:, 128 * c : 128 * (c + 1)] = hit.astype(BF16)
            at_row = lax.broadcasted_iota(jnp.int32, (total_rows, 128), 0)
            i0 = lax.broadcasted_iota(jnp.int32, (128, 128), 0)
            i1 = lax.broadcasted_iota(jnp.int32, (128, 128), 1)
            for c in range(count // 128):
                part = jnp.where(i0 == i1, wanted[128 * c : 128 * (c + 1)], 0)
                along = jnp.sum(part, axis=0, keepdims=True)
                hit = jnp.where(at_row == along, 1.0, 0.0)
                amat[:, 128 * c : 128 * (c + 1)] = hit.astype(BF16)
        z_gather.wait()
        shares = zg[k].reshape(nz * 16, 128)
        picked = jnp.dot(bmat[...], shares, preferred_element_type=F32)
        ys[k] = picked.astype(BF16).reshape(members, 16, 128)
        rg[k, me] = ys[k, me]
        answer = exchange("p", lambda i, k=k: ys.at[k, i], lambda i, k=k: rg.at[k, i])
        user_gather.wait()
        for s in range(slots):
            total = jnp.zeros((64, 256), F32)
            for p in range(nr):
                total += gu[k, p].astype(F32) * (rows[s] == p).astype(jnp.int32).astype(F32)
            ub[s] = total.astype(BF16)
        user_t[...] = jnp.zeros_like(user_t)
        if last:
            ctx_t[...] = jnp.zeros_like(ctx_t)
        else:
            load.wait()
        answer.wait()
        got = rg[k].astype(F32)
        for s in range(slots):
            vf[s] = join_shares(got[:, 4 * s : 4 * s + 4, :])

        @pl.loop(0, 8)
        def _(c):
            for s in range(slots):
                u, w = ub[s], wf[s]
                v = vf[s, pl.ds(pl.multiple_of(c * 8, 8), 8), :]
                pair = (v[:, None, :] * w[None, :, :]).astype(BF16).reshape(512, 256)
                model = lax.dot_general(
                    u, pair, (((1,), (1,)), ((), ())), preferred_element_type=F32
                )
                x = xb[s, :, pl.ds(pl.multiple_of(c * 512, 512), 512)]
                resid = (model - x.astype(F32)).astype(BF16)
                user_t[s] += jnp.dot(resid, pair, preferred_element_type=F32)
                g = lax.dot_general(
                    resid, u, (((0,), (0,)), ((), ())), preferred_element_type=F32
                ).reshape(8, 64, 256)
                item_t[s, pl.ds(pl.multiple_of(c * 8, 8), 8), :] = jnp.sum(g * w[None], axis=1)
                if last:
                    ctx_t[s] += jnp.sum(g * v[:, None, :], axis=0)

        xs, xr = (xs1, xr1) if last else (xs0, xr0)
        tiles = [to_tiles(item_t[s]) for s in range(slots)]
        fill = jnp.zeros((16, 4, 128), F32)
        for half in range(2):
            cut = [t[:, 4 * half : 4 * half + 4] for t in tiles]
            part = jnp.concatenate(cut + [fill], axis=1).astype(BF16)
            for v in range(16):
                xs[2 * v + half, pl.ds(0, 16), :] = part[v]
        if last:
            for c in range(2):
                total = jnp.zeros((64, 256), F32)
                for s in range(slots):
                    mine = alive[s] * (ctxs[s] == c).astype(jnp.int32)
                    total += ctx_t[s] * mine.astype(F32)
                part = to_tiles(total)
                part = jnp.concatenate([part, jnp.zeros_like(part)], axis=1).astype(BF16)
                xs[pl.ds(16 * c, 16), pl.ds(16, 16), :] = part
        xr[me] = xs[me]
        item_parts = exchange("p", lambda i, xs=xs: xs.at[i], lambda i, xr=xr: xr.at[i])
        for p in range(nr):
            total = jnp.zeros((64, 256), F32)
            for s in range(slots):
                mine = alive[s] * (rows[s] == p).astype(jnp.int32)
                total += user_t[s] * mine.astype(F32)
            us[k, p] = total.astype(BF16)
        ur[k, r] = us[k, r]
        user_parts = exchange("r", lambda i, k=k: us.at[k, i], lambda i, k=k: ur.at[k, i])

        item_parts.wait()
        parts = xr[:, :16, :].reshape(members * 16, 128)
        summed = jnp.dot(amat[...], parts, preferred_element_type=F32)
        zs[k] = summed.astype(BF16).reshape(nz, 16, 128)
        zr[k, z] = zs[k, z]
        z_parts = exchange("z", lambda i, k=k: zs.at[k, i], lambda i, k=k: zr.at[k, i])
        if last:
            cz[z] = jnp.sum(xr[:, 16:, :].astype(F32), axis=0)[:8]
            ctx_z = exchange("z", lambda i: cz.at[z], lambda i: cz.at[i])
        user_parts.wait()
        user_own = user_own - user_step * jnp.sum(ur[k].astype(F32), axis=0)
        if last:
            new_users[...] = user_own
        else:
            gu[k + 1, r] = user_own.astype(BF16)
            user_gather = exchange(
                "r", lambda i, k=k: gu.at[k + 1, r], lambda i, k=k: gu.at[k + 1, i]
            )
        z_parts.wait()
        item_delta = item_delta + item_step * jnp.sum(zr[k].astype(F32), axis=0)
        if not last:
            zg[k + 1, z] = (item_own - item_delta).astype(BF16)

    ctx_z.wait()
    ctx_share = jnp.sum(cz[...], axis=0) * grad_scale
    for i in range(NQ):
        part = item_delta[4 * i : 4 * i + 4]
        fs[i] = jnp.concatenate([part, part, ctx_share], axis=0).astype(BF16)
    fin[me] = fs[q]
    final = exchange("p", lambda i: fs.at[i // nr], lambda i: fin.at[i])
    final.wait()
    got = fin[...].astype(F32)
    new_items[...] = item_in[...] - join_shares(got[:, :4])
    for c in range(2):
        ctx_out[pl.ds(64 * c, 64), :] = from_tiles(got[16 * c : 16 * c + 16, 8:])
    for e in pending:
        e.finish()


def local(
    blocks, block_row, block_col, block_ctx, live_blocks, user_factor, item_factor, context_factor
):
    nr = lax.axis_size("rows")
    nz = lax.axis_size("blk") // NQ
    slots = blocks.shape[2]
    nb = nz * NQ
    edge = blocks.shape[3]
    vm = pltpu.VMEM
    dma = pltpu.SemaphoreType.DMA
    members = NQ * nr
    scratch = [
        vm((slots, 64, 4096), BF16),
        vm((ITERS, nr, 64, 256), BF16),
        vm((members, 8, 128), jnp.int32),
        vm((members * 16, nz * 16), BF16),
        vm((nz * 16, members * 16), BF16),
        vm((NQ, 8, 128), F32),
        vm((members, 8, 128), F32),
        vm((ITERS, nz, 16, 128), BF16),
        vm((ITERS, members, 16, 128), BF16),
        vm((ITERS, members, 16, 128), BF16),
        vm((slots, 64, 256), F32),
        vm((slots, 64, 256), F32),
        vm((slots, 64, 256), BF16),
        vm((slots, 64, 256), F32),
        vm((slots, 64, 256), F32),
        vm((slots, 64, 256), F32),
        vm((members, 16, 128), BF16),
        vm((members, 16, 128), BF16),
        vm((members, 32, 128), BF16),
        vm((members, 32, 128), BF16),
        vm((ITERS, nr, 64, 256), BF16),
        vm((ITERS, nr, 64, 256), BF16),
        vm((ITERS, nz, 16, 128), BF16),
        vm((ITERS, nz, 16, 128), BF16),
        vm((nz, 8, 128), F32),
        vm((NQ, 16, 128), BF16),
        vm((members, 16, 128), BF16),
        pltpu.SMEM((1, 1, slots), jnp.int32),
        pltpu.SMEM((1, 1, slots), jnp.int32),
        pltpu.SMEM((1, 1, slots), jnp.int32),
        pltpu.SMEM((1, 1), jnp.int32),
        vm((64, 256), F32),
        vm((64, 256), F32),
        vm((128, 256), F32),
        dma((7,)),
        dma,
        dma((4, nr - 1)),
        dma((4, nr - 1)),
        dma((1, NQ - 1)),
        dma((1, NQ - 1)),
        dma((5, nz - 1)),
        dma((5, nz - 1)),
        dma((6, members - 1)),
        dma((6, members - 1)),
    ]
    body = functools.partial(
        kernel,
        nz,
        nr,
        6.4 / (edge * edge),
        16.0 / (edge * edge * nr),
        8.0 / (edge * math.sqrt(nb * nr)),
    )
    in_vmem = pl.BlockSpec(memory_space=pltpu.VMEM)
    return pl.pallas_call(
        body,
        out_shape=(
            jax.ShapeDtypeStruct(user_factor.shape, F32),
            jax.ShapeDtypeStruct(item_factor.shape, F32),
            jax.ShapeDtypeStruct(context_factor.shape, F32),
        ),
        in_specs=[pl.BlockSpec(memory_space=pltpu.HBM)] * 8,
        out_specs=(in_vmem,) * 3,
        scratch_shapes=scratch,
        compiler_params=pltpu.CompilerParams(
            collective_id=0, has_side_effects=True, vmem_limit_bytes=56 * 1024 * 1024
        ),
    )(
        blocks, block_row, block_col, block_ctx, live_blocks,
        user_factor, item_factor, context_factor,
    )


def solution(mesh):
    return jax.shard_map(
        local,
        mesh=mesh,
        in_specs=(
            P("blk", "rows", None, None, None),
            P("blk", "rows", None),
            P("blk", "rows", None),
            P("blk", "rows", None),
            P("blk", "rows"),
            P(("blk", "rows"), None),
            P("blk", None),
            P(),
        ),
        out_specs=(P(("blk", "rows"), None), P("blk", None), P()),
        check_vma=False,
    )
```

time: 135 us -> 113 us (0.84)
  Pallas kernels: 126 us -> 107 us
  local copies, waits for them, and re-layouts: 7.86 us -> 4.51 us
    pallas_call x1, Pallas kernels: 126 us -> 107 us  [local(): pl.pallas_call(body, out_shape=(jax.ShapeDtypeStruct(user_factor.shape, F...]
    unnamed x17 -> x3, local copies, waits for them, and re-layouts: 7.86 us -> 4.51 us
where the time goes in v2:
time: 113 us
  Pallas kernels  107 us (95%)
  local copies, waits for them, and re-layouts  4.51 us (4%)
  between operations  1.29 us (1%)
    pallas_call x1, Pallas kernels, local(): pl.pallas_call(body, out_shape=(jax.ShapeDtypeStruct(user_factor.shape, F...  107 us
    unnamed x3, local copies, waits for them, and re-layouts  4.51 us

profile of v2, /device:TPU:1, one launch (start us, length us, event | category | flops | bytes accessed | tf_op | source)
XLA Modules:
  0.0 112.8 jit_solution(2375819780479375021)
XLA Ops:
  1.3 107.0 %shard_map.103 = (f32[64,256]{1,0:T(8,128)}, f32[64,256]{1,0:T(8,128)}, f32[128,256]{1,0:T(8,128)}) custom-call(bf16[1,1,3,64,4096]{4,3,2,1,0:T(8,128)(2,1)} %blocks.1, s32[1,1,3]{2,1,0:T(1,128)} %row_hbm.1, s32[1,1,3]{2,1,0:T(1,128)} %col_hbm.1, s32[1,1,3]{2,1,0:T(1,128)} %ctx_hbm.1, s32[1,1]{1,0:T(1,128)S(6)} %copy.14.live_hbm, f32[64,256]{1,0:T(8,128)} %user_hbm.1, ...), custom_call_target="tpu_custom_call" | custom-call | tf_op jit(solution)/shard_map/pallas_call | solution.py:407
  108.3 1.5 %copy.15 = f32[64,256]{1,0:T(8,128)} copy(f32[64,256]{1,0:T(8,128)} %get-tuple-element.6) | data formatting | bytes 131072
  109.8 1.5 %copy.16 = f32[64,256]{1,0:T(8,128)} copy(f32[64,256]{1,0:T(8,128)} %get-tuple-element.7) | data formatting | bytes 131072
  111.3 1.6 %copy.17 = f32[128,256]{1,0:T(8,128)} copy(f32[128,256]{1,0:T(8,128)} %get-tuple-element.8) | data formatting | bytes 262144

commit v3 on v2

--- a/solution.py
+++ b/solution.py
@@ -16,46 +16,39 @@
 
 
 class Exchange:
-    def __init__(self, group, src, land, send, recv):
-        self.steps, self.me, self.peer, self.source, self.dev = group
-        self.src, self.land, self.send, self.recv = src, land, send, recv
-
-    def _copy(self, i):
-        to = self.peer(i)
-        return pltpu.make_async_remote_copy(
-            src_ref=self.src(to),
-            dst_ref=self.land(self.me),
-            send_sem=self.send.at[i],
-            recv_sem=self.recv.at[i],
-            device_id=self.dev(to),
-            device_id_type=MESH,
-        )
-
-    def _arrival(self, i):
-        frm = self.source(i)
-        return pltpu.make_async_remote_copy(
-            src_ref=self.land(frm),
-            dst_ref=self.land(frm),
-            send_sem=self.send.at[i],
-            recv_sem=self.recv.at[i],
-            device_id=self.dev(frm),
-            device_id_type=MESH,
-        )
+    def __init__(self, group, src, land, whole, send, recv):
+        self.steps, self.me, self.peer, self.dev = group
+        self.src, self.land, self.whole, self.send, self.recv = src, land, whole, send, recv
 
     def start(self):
         @pl.loop(0, self.steps)
         def _(i):
-            self._copy(i).start()
+            to = self.peer(i)
+            pltpu.make_async_remote_copy(
+                src_ref=self.src(to),
+                dst_ref=self.land(self.me),
+                send_sem=self.send,
+                recv_sem=self.recv,
+                device_id=self.dev(to),
+                device_id_type=MESH,
+            ).start()
+
+    def _all(self):
+        part = self.whole.at[pl.ds(0, self.steps)]
+        return pltpu.make_async_remote_copy(
+            src_ref=part,
+            dst_ref=part,
+            send_sem=self.send,
+            recv_sem=self.recv,
+            device_id=self.dev(self.peer(0)),
+            device_id_type=MESH,
+        )
 
     def wait(self):
-        @pl.loop(0, self.steps)
-        def _(i):
-            self._arrival(i).wait_recv()
+        self._all().wait_recv()
 
     def finish(self):
-        @pl.loop(0, self.steps)
-        def _(i):
-            self._copy(i).wait_send()
+        self._all().wait_send()
 
 
 def ring(n, me, dev, far_first):
@@ -68,7 +61,6 @@
         n - 1,
         me,
         lambda i: lax.rem(me + offset(i), n),
-        lambda i: lax.rem(me + n - offset(i), n),
         dev,
     )
 
@@ -77,17 +69,17 @@
     y_lo, core, y_hi, x = q // 2, lax.rem(q, 2), r // 4, lax.rem(r, 4)
     n = NQ * nr
 
-    def member(i, sign):
+    def member(i):
         t = n - 1 - i
         b = (t // 4) % 4
         dx = (3 * b + 3 * (b // 2) - 2 * (b // 3)) % 4
-        to_x = lax.rem(x + 4 + sign * dx, 4)
+        to_x = lax.rem(x + dx, 4)
         to_hi = lax.rem(y_hi + t // 16, 2)
         to_lo = lax.rem(y_lo + (t // 2) % 2, 2)
         to_core = lax.rem(core + t % 2, 2)
         return (to_lo * 2 + to_core) * nr + to_hi * 4 + to_x
 
-    return (n - 1, q * nr + r, lambda i: member(i, 1), lambda i: member(i, -1), dev)
+    return (n - 1, q * nr + r, member, dev)
 
 
 def to_tiles(x):
@@ -133,18 +125,18 @@
     pending = []
     used = {"r": 0, "q": 0, "z": 0, "p": 0}
 
-    def exchange(kind, src, land):
+    def exchange(kind, src, land, whole):
         send, recv = semaphores[kind]
         at = used[kind]
         used[kind] += 1
-        e = Exchange(groups[kind], src, land, send.at[at], recv.at[at])
+        e = Exchange(groups[kind], src, land, whole, send.at[at], recv.at[at])
         e.start()
         pending.append(e)
         return e
 
     barrier = pltpu.get_barrier_semaphore()
     for kind in ("z", "p"):
-        steps, _, peer, _, dev = groups[kind]
+        steps, _, peer, dev = groups[kind]
 
         @pl.loop(0, steps)
         def _(i):
@@ -192,8 +184,8 @@
 
     pl.semaphore_wait(barrier, nz - 1 + members - 1)
 
-    item_first = exchange("q", lambda i: ist.at[i * nr + r], lambda i: iq.at[i])
-    index_gather = exchange("p", lambda i: idx.at[me], lambda i: idx.at[i])
+    item_first = exchange("q", lambda i: ist.at[i * nr + r], lambda i: iq.at[i], iq)
+    index_gather = exchange("p", lambda i: idx.at[me], lambda i: idx.at[i], idx)
     item_first.wait()
     item_own = jnp.concatenate([iq[i][:4] for i in range(NQ)], axis=0)
     item_delta = jnp.zeros((16, 128), F32)
@@ -201,9 +193,9 @@
 
     for k in range(ITERS):
         last = k == ITERS - 1
-        z_gather = exchange("z", lambda i, k=k: zg.at[k, z], lambda i, k=k: zg.at[k, i])
+        z_gather = exchange("z", lambda i, k=k: zg.at[k, z], lambda i, k=k: zg.at[k, i], zg.at[k])
         if k == 0:
-            user_gather = exchange("r", lambda i: gu.at[0, r], lambda i: gu.at[0, i])
+            user_gather = exchange("r", lambda i: gu.at[0, r], lambda i: gu.at[0, i], gu.at[0])
             for s in range(slots):
                 w = ctx_in[...].astype(BF16).astype(F32)
                 second = ctxs[s].astype(F32)
@@ -235,7 +227,7 @@
         picked = jnp.dot(bmat[...], shares, preferred_element_type=F32)
         ys[k] = picked.astype(BF16).reshape(members, 16, 128)
         rg[k, me] = ys[k, me]
-        answer = exchange("p", lambda i, k=k: ys.at[k, i], lambda i, k=k: rg.at[k, i])
+        answer = exchange("p", lambda i, k=k: ys.at[k, i], lambda i, k=k: rg.at[k, i], rg.at[k])
         user_gather.wait()
         for s in range(slots):
             total = jnp.zeros((64, 256), F32)
@@ -289,7 +281,7 @@
                 part = jnp.concatenate([part, jnp.zeros_like(part)], axis=1).astype(BF16)
                 xs[pl.ds(16 * c, 16), pl.ds(16, 16), :] = part
         xr[me] = xs[me]
-        item_parts = exchange("p", lambda i, xs=xs: xs.at[i], lambda i, xr=xr: xr.at[i])
+        item_parts = exchange("p", lambda i, xs=xs: xs.at[i], lambda i, xr=xr: xr.at[i], xr)
         for p in range(nr):
             total = jnp.zeros((64, 256), F32)
             for s in range(slots):
@@ -297,17 +289,17 @@
                 total += user_t[s] * mine.astype(F32)
             us[k, p] = total.astype(BF16)
         ur[k, r] = us[k, r]
-        user_parts = exchange("r", lambda i, k=k: us.at[k, i], lambda i, k=k: ur.at[k, i])
+        user_parts = exchange("r", lambda i, k=k: us.at[k, i], lambda i, k=k: ur.at[k, i], ur.at[k])
 
         item_parts.wait()
         parts = xr[:, :16, :].reshape(members * 16, 128)
         summed = jnp.dot(amat[...], parts, preferred_element_type=F32)
         zs[k] = summed.astype(BF16).reshape(nz, 16, 128)
         zr[k, z] = zs[k, z]
-        z_parts = exchange("z", lambda i, k=k: zs.at[k, i], lambda i, k=k: zr.at[k, i])
+        z_parts = exchange("z", lambda i, k=k: zs.at[k, i], lambda i, k=k: zr.at[k, i], zr.at[k])
         if last:
             cz[z] = jnp.sum(xr[:, 16:, :].astype(F32), axis=0)[:8]
-            ctx_z = exchange("z", lambda i: cz.at[z], lambda i: cz.at[i])
+            ctx_z = exchange("z", lambda i: cz.at[z], lambda i: cz.at[i], cz)
         user_parts.wait()
         user_own = user_own - user_step * jnp.sum(ur[k].astype(F32), axis=0)
         if last:
@@ -315,8 +307,7 @@
         else:
             gu[k + 1, r] = user_own.astype(BF16)
             user_gather = exchange(
-                "r", lambda i, k=k: gu.at[k + 1, r], lambda i, k=k: gu.at[k + 1, i]
-            )
+                "r", lambda i, k=k: gu.at[k + 1, r], lambda i, k=k: gu.at[k + 1, i], gu.at[k + 1])
         z_parts.wait()
         item_delta = item_delta + item_step * jnp.sum(zr[k].astype(F32), axis=0)
         if not last:
@@ -326,12 +317,13 @@
     ctx_share = jnp.sum(cz[...], axis=0) * grad_scale
     for i in range(NQ):
         part = item_delta[4 * i : 4 * i + 4]
-        fs[i] = jnp.concatenate([part, part, ctx_share], axis=0).astype(BF16)
+        rest = part - part.astype(BF16).astype(F32)
+        fs[i] = jnp.concatenate([part, rest, ctx_share], axis=0).astype(BF16)
     fin[me] = fs[q]
-    final = exchange("p", lambda i: fs.at[i // nr], lambda i: fin.at[i])
+    final = exchange("p", lambda i: fs.at[i // nr], lambda i: fin.at[i], fin)
     final.wait()
     got = fin[...].astype(F32)
-    new_items[...] = item_in[...] - join_shares(got[:, :4])
+    new_items[...] = item_in[...] - join_shares(got[:, :4] + got[:, 4:8])
     for c in range(2):
         ctx_out[pl.ds(64 * c, 64), :] = from_tiles(got[16 * c : 16 * c + 16, 8:])
     for e in pending:
@@ -386,14 +378,14 @@
         vm((128, 256), F32),
         dma((7,)),
         dma,
-        dma((4, nr - 1)),
-        dma((4, nr - 1)),
-        dma((1, NQ - 1)),
-        dma((1, NQ - 1)),
-        dma((5, nz - 1)),
-        dma((5, nz - 1)),
-        dma((6, members - 1)),
-        dma((6, members - 1)),
+        dma((4,)),
+        dma((4,)),
+        dma((1,)),
+        dma((1,)),
+        dma((5,)),
+        dma((5,)),
+        dma((6,)),
+        dma((6,)),
     ]
     body = functools.partial(
         kernel,

time: 113 us -> 106 us (0.938)
  Pallas kernels: 107 us -> 99.7 us
    pallas_call x1, Pallas kernels: 107 us -> 99.7 us  [local(): pl.pallas_call(body, out_shape=(jax.ShapeDtypeStruct(user_factor.shape, F...]
where the time goes in v3:
time: 106 us
  Pallas kernels  99.7 us (94%)
  local copies, waits for them, and re-layouts  4.51 us (4%)
  between operations  1.29 us (1%)
    pallas_call x1, Pallas kernels, local(): pl.pallas_call(body, out_shape=(jax.ShapeDtypeStruct(user_factor.shape, F...  99.7 us
    unnamed x3, local copies, waits for them, and re-layouts  4.51 us

profile of v3, /device:TPU:1, one launch (start us, length us, event | category | flops | bytes accessed | tf_op | source)
XLA Modules:
  0.0 105.5 jit_solution(9295506923869059948)
XLA Ops:
  1.3 99.7 %shard_map.103 = (f32[64,256]{1,0:T(8,128)}, f32[64,256]{1,0:T(8,128)}, f32[128,256]{1,0:T(8,128)}) custom-call(bf16[1,1,3,64,4096]{4,3,2,1,0:T(8,128)(2,1)} %blocks.1, s32[1,1,3]{2,1,0:T(1,128)} %row_hbm.1, s32[1,1,3]{2,1,0:T(1,128)} %col_hbm.1, s32[1,1,3]{2,1,0:T(1,128)} %ctx_hbm.1, s32[1,1]{1,0:T(1,128)S(6)} %copy.14.live_hbm, f32[64,256]{1,0:T(8,128)} %user_hbm.1, ...), custom_call_target="tpu_custom_call" | custom-call | tf_op jit(solution)/shard_map/pallas_call | solution.py:399
  101.0 1.5 %copy.15 = f32[64,256]{1,0:T(8,128)} copy(f32[64,256]{1,0:T(8,128)} %get-tuple-element.6) | data formatting | bytes 131072
  102.5 1.5 %copy.16 = f32[64,256]{1,0:T(8,128)} copy(f32[64,256]{1,0:T(8,128)} %get-tuple-element.7) | data formatting | bytes 131072
  104.0 1.6 %copy.17 = f32[128,256]{1,0:T(8,128)} copy(f32[128,256]{1,0:T(8,128)} %get-tuple-element.8) | data formatting | bytes 262144

commit v4 on v3

--- a/solution.py
+++ b/solution.py
@@ -21,8 +21,7 @@
         self.src, self.land, self.whole, self.send, self.recv = src, land, whole, send, recv
 
     def start(self):
-        @pl.loop(0, self.steps)
-        def _(i):
+        for i in range(self.steps):
             to = self.peer(i)
             pltpu.make_async_remote_copy(
                 src_ref=self.src(to),
@@ -69,15 +68,23 @@
     y_lo, core, y_hi, x = q // 2, lax.rem(q, 2), r // 4, lax.rem(r, 4)
     n = NQ * nr
 
+    xs = [lax.rem(x + d, 4) for d in range(4)]
+    his = [y_hi * 4, (1 - y_hi) * 4]
+    qs = [
+        (lo * 2 + c) * nr for lo in (y_lo, 1 - y_lo) for c in (core, 1 - core)
+    ]
+    rows = [hi + xx for hi in his for xx in xs]
+    hops = [(dhi * 2 if not dlo else 1) + min(d, 4 - d) + dlo * (1 - dhi)
+            for dlo in range(2) for dhi in range(2) for d in range(4)]
+    order = sorted(
+        (-hops[(dlo * 2 + dhi) * 4 + d], dlo * 2 + c, dhi * 4 + d)
+        for dlo in range(2) for c in range(2) for dhi in range(2) for d in range(4)
+    )
+    steps = [(a, b) for _, a, b in order if (a, b) != (0, 0)]
+
     def member(i):
-        t = n - 1 - i
-        b = (t // 4) % 4
-        dx = (3 * b + 3 * (b // 2) - 2 * (b // 3)) % 4
-        to_x = lax.rem(x + dx, 4)
-        to_hi = lax.rem(y_hi + t // 16, 2)
-        to_lo = lax.rem(y_lo + (t // 2) % 2, 2)
-        to_core = lax.rem(core + t % 2, 2)
-        return (to_lo * 2 + to_core) * nr + to_hi * 4 + to_x
+        a, b = steps[i]
+        return qs[a] + rows[b]
 
     return (n - 1, q * nr + r, member, dev)
 
@@ -138,8 +145,7 @@
     for kind in ("z", "p"):
         steps, _, peer, dev = groups[kind]
 
-        @pl.loop(0, steps)
-        def _(i):
+        for i in range(steps):
             pl.semaphore_signal(
                 barrier, inc=1, device_id=dev(peer(i)), device_id_type=MESH
             )
@@ -244,22 +250,22 @@
         for s in range(slots):
             vf[s] = join_shares(got[:, 4 * s : 4 * s + 4, :])
 
-        @pl.loop(0, 8)
+        @pl.loop(0, 2)
         def _(c):
             for s in range(slots):
                 u, w = ub[s], wf[s]
-                v = vf[s, pl.ds(pl.multiple_of(c * 8, 8), 8), :]
-                pair = (v[:, None, :] * w[None, :, :]).astype(BF16).reshape(512, 256)
+                v = vf[s, pl.ds(pl.multiple_of(c * 32, 32), 32), :]
+                pair = (v[:, None, :] * w[None, :, :]).astype(BF16).reshape(2048, 256)
                 model = lax.dot_general(
                     u, pair, (((1,), (1,)), ((), ())), preferred_element_type=F32
                 )
-                x = xb[s, :, pl.ds(pl.multiple_of(c * 512, 512), 512)]
+                x = xb[s, :, pl.ds(pl.multiple_of(c * 2048, 2048), 2048)]
                 resid = (model - x.astype(F32)).astype(BF16)
                 user_t[s] += jnp.dot(resid, pair, preferred_element_type=F32)
                 g = lax.dot_general(
                     resid, u, (((0,), (0,)), ((), ())), preferred_element_type=F32
-                ).reshape(8, 64, 256)
-                item_t[s, pl.ds(pl.multiple_of(c * 8, 8), 8), :] = jnp.sum(g * w[None], axis=1)
+                ).reshape(32, 64, 256)
+                item_t[s, pl.ds(pl.multiple_of(c * 32, 32), 32), :] = jnp.sum(g * w[None], axis=1)
                 if last:
                     ctx_t[s] += jnp.sum(g * v[:, None, :], axis=0)
 

time: 106 us -> 97.8 us (0.923)
  Pallas kernels: 99.7 us -> 91.8 us
    pallas_call x1, Pallas kernels: 99.7 us -> 91.8 us  [local(): pl.pallas_call(body, out_shape=(jax.ShapeDtypeStruct(user_factor.shape, F...]
where the time goes in v4:
time: 97.8 us; the launch traced here: 97.6 us
  Pallas kernels  91.8 us (94%)
  local copies, waits for them, and re-layouts  4.51 us (5%)
  between operations  1.29 us (1%)
    pallas_call x1, Pallas kernels, local(): pl.pallas_call(body, out_shape=(jax.ShapeDtypeStruct(user_factor.shape, F...  91.8 us
    unnamed x3, local copies, waits for them, and re-layouts  4.51 us

profile of v4, /device:TPU:1, one launch (start us, length us, event | category | flops | bytes accessed | tf_op | source)
XLA Modules:
  0.0 97.6 jit_solution(7494116511514535926)
XLA Ops:
  1.3 91.8 %shard_map.103 = (f32[64,256]{1,0:T(8,128)}, f32[64,256]{1,0:T(8,128)}, f32[128,256]{1,0:T(8,128)}) custom-call(bf16[1,1,3,64,4096]{4,3,2,1,0:T(8,128)(2,1)} %blocks.1, s32[1,1,3]{2,1,0:T(1,128)} %row_hbm.1, s32[1,1,3]{2,1,0:T(1,128)} %col_hbm.1, s32[1,1,3]{2,1,0:T(1,128)} %ctx_hbm.1, s32[1,1]{1,0:T(1,128)S(6)} %copy.14.live_hbm, f32[64,256]{1,0:T(8,128)} %user_hbm.1, ...), custom_call_target="tpu_custom_call" | custom-call | tf_op jit(solution)/shard_map/pallas_call | solution.py:405
  93.0 1.5 %copy.15 = f32[64,256]{1,0:T(8,128)} copy(f32[64,256]{1,0:T(8,128)} %get-tuple-element.6) | data formatting | bytes 131072
  94.5 1.5 %copy.16 = f32[64,256]{1,0:T(8,128)} copy(f32[64,256]{1,0:T(8,128)} %get-tuple-element.7) | data formatting | bytes 131072
  96.0 1.6 %copy.17 = f32[128,256]{1,0:T(8,128)} copy(f32[128,256]{1,0:T(8,128)} %get-tuple-element.8) | data formatting | bytes 262144

commit v5 on v4

--- a/solution.py
+++ b/solution.py
@@ -250,22 +250,22 @@
         for s in range(slots):
             vf[s] = join_shares(got[:, 4 * s : 4 * s + 4, :])
 
-        @pl.loop(0, 2)
+        @pl.loop(0, 1)
         def _(c):
             for s in range(slots):
                 u, w = ub[s], wf[s]
-                v = vf[s, pl.ds(pl.multiple_of(c * 32, 32), 32), :]
-                pair = (v[:, None, :] * w[None, :, :]).astype(BF16).reshape(2048, 256)
+                v = vf[s, pl.ds(pl.multiple_of(c * 64, 64), 64), :]
+                pair = (v.astype(BF16)[:, None, :] * w.astype(BF16)[None, :, :]).reshape(4096, 256)
                 model = lax.dot_general(
                     u, pair, (((1,), (1,)), ((), ())), preferred_element_type=F32
                 )
-                x = xb[s, :, pl.ds(pl.multiple_of(c * 2048, 2048), 2048)]
+                x = xb[s, :, pl.ds(pl.multiple_of(c * 4096, 4096), 4096)]
                 resid = (model - x.astype(F32)).astype(BF16)
                 user_t[s] += jnp.dot(resid, pair, preferred_element_type=F32)
                 g = lax.dot_general(
                     resid, u, (((0,), (0,)), ((), ())), preferred_element_type=F32
-                ).reshape(32, 64, 256)
-                item_t[s, pl.ds(pl.multiple_of(c * 32, 32), 32), :] = jnp.sum(g * w[None], axis=1)
+                ).reshape(64, 64, 256)
+                item_t[s, pl.ds(pl.multiple_of(c * 64, 64), 64), :] = jnp.sum(g * w[None], axis=1)
                 if last:
                     ctx_t[s] += jnp.sum(g * v[:, None, :], axis=0)
 

time: 97.8 us -> 97.3 us (level)
  no operation moved by 1% of the time
where the time goes in v5:
time: 97.3 us; the launch traced here: 97 us
  Pallas kernels  91.2 us (94%)
  local copies, waits for them, and re-layouts  4.51 us (5%)
  between operations  1.29 us (1%)
    pallas_call x1, Pallas kernels, local(): pl.pallas_call(body, out_shape=(jax.ShapeDtypeStruct(user_factor.shape, F...  91.2 us
    unnamed x3, local copies, waits for them, and re-layouts  4.51 us

profile of v5, /device:TPU:1, one launch (start us, length us, event | category | flops | bytes accessed | tf_op | source)
XLA Modules:
  0.0 97.0 jit_solution(7799135769204172732)
XLA Ops:
  1.3 91.2 %shard_map.103 = (f32[64,256]{1,0:T(8,128)}, f32[64,256]{1,0:T(8,128)}, f32[128,256]{1,0:T(8,128)}) custom-call(bf16[1,1,3,64,4096]{4,3,2,1,0:T(8,128)(2,1)} %blocks.1, s32[1,1,3]{2,1,0:T(1,128)} %row_hbm.1, s32[1,1,3]{2,1,0:T(1,128)} %col_hbm.1, s32[1,1,3]{2,1,0:T(1,128)} %ctx_hbm.1, s32[1,1]{1,0:T(1,128)S(6)} %copy.14.live_hbm, f32[64,256]{1,0:T(8,128)} %user_hbm.1, ...), custom_call_target="tpu_custom_call" | custom-call | tf_op jit(solution)/shard_map/pallas_call | solution.py:405
  92.5 1.5 %copy.15 = f32[64,256]{1,0:T(8,128)} copy(f32[64,256]{1,0:T(8,128)} %get-tuple-element.6) | data formatting | bytes 131072
  94.0 1.5 %copy.16 = f32[64,256]{1,0:T(8,128)} copy(f32[64,256]{1,0:T(8,128)} %get-tuple-element.7) | data formatting | bytes 131072
  95.4 1.6 %copy.17 = f32[128,256]{1,0:T(8,128)} copy(f32[128,256]{1,0:T(8,128)} %get-tuple-element.8) | data formatting | bytes 262144

commit v6 on v5

--- a/solution.py
+++ b/solution.py
@@ -288,15 +288,6 @@
                 xs[pl.ds(16 * c, 16), pl.ds(16, 16), :] = part
         xr[me] = xs[me]
         item_parts = exchange("p", lambda i, xs=xs: xs.at[i], lambda i, xr=xr: xr.at[i], xr)
-        for p in range(nr):
-            total = jnp.zeros((64, 256), F32)
-            for s in range(slots):
-                mine = alive[s] * (rows[s] == p).astype(jnp.int32)
-                total += user_t[s] * mine.astype(F32)
-            us[k, p] = total.astype(BF16)
-        ur[k, r] = us[k, r]
-        user_parts = exchange("r", lambda i, k=k: us.at[k, i], lambda i, k=k: ur.at[k, i], ur.at[k])
-
         item_parts.wait()
         parts = xr[:, :16, :].reshape(members * 16, 128)
         summed = jnp.dot(amat[...], parts, preferred_element_type=F32)
@@ -306,6 +297,14 @@
         if last:
             cz[z] = jnp.sum(xr[:, 16:, :].astype(F32), axis=0)[:8]
             ctx_z = exchange("z", lambda i: cz.at[z], lambda i: cz.at[i], cz)
+        for p in range(nr):
+            total = jnp.zeros((64, 256), F32)
+            for s in range(slots):
+                mine = alive[s] * (rows[s] == p).astype(jnp.int32)
+                total += user_t[s] * mine.astype(F32)
+            us[k, p] = total.astype(BF16)
+        ur[k, r] = us[k, r]
+        user_parts = exchange("r", lambda i, k=k: us.at[k, i], lambda i, k=k: ur.at[k, i], ur.at[k])
         user_parts.wait()
         user_own = user_own - user_step * jnp.sum(ur[k].astype(F32), axis=0)
         if last:

time: 97.3 us -> 95.7 us (0.984)
  Pallas kernels: 91.2 us -> 89.6 us
    pallas_call x1, Pallas kernels: 91.2 us -> 89.6 us  [local(): pl.pallas_call(body, out_shape=(jax.ShapeDtypeStruct(user_factor.shape, F...]
where the time goes in v6:
time: 95.7 us; the launch traced here: 95.4 us
  Pallas kernels  89.6 us (94%)
  local copies, waits for them, and re-layouts  4.51 us (5%)
  between operations  1.29 us (1%)
    pallas_call x1, Pallas kernels, local(): pl.pallas_call(body, out_shape=(jax.ShapeDtypeStruct(user_factor.shape, F...  89.6 us
    unnamed x3, local copies, waits for them, and re-layouts  4.51 us

profile of v6, /device:TPU:1, one launch (start us, length us, event | category | flops | bytes accessed | tf_op | source)
XLA Modules:
  0.0 95.4 jit_solution(17463232851495858943)
XLA Ops:
  1.3 89.6 %shard_map.103 = (f32[64,256]{1,0:T(8,128)}, f32[64,256]{1,0:T(8,128)}, f32[128,256]{1,0:T(8,128)}) custom-call(bf16[1,1,3,64,4096]{4,3,2,1,0:T(8,128)(2,1)} %blocks.1, s32[1,1,3]{2,1,0:T(1,128)} %row_hbm.1, s32[1,1,3]{2,1,0:T(1,128)} %col_hbm.1, s32[1,1,3]{2,1,0:T(1,128)} %ctx_hbm.1, s32[1,1]{1,0:T(1,128)S(6)} %copy.14.live_hbm, f32[64,256]{1,0:T(8,128)} %user_hbm.1, ...), custom_call_target="tpu_custom_call" | custom-call | tf_op jit(solution)/shard_map/pallas_call | solution.py:404
  90.9 1.5 %copy.15 = f32[64,256]{1,0:T(8,128)} copy(f32[64,256]{1,0:T(8,128)} %get-tuple-element.6) | data formatting | bytes 131072
  92.4 1.5 %copy.16 = f32[64,256]{1,0:T(8,128)} copy(f32[64,256]{1,0:T(8,128)} %get-tuple-element.7) | data formatting | bytes 131072
  93.9 1.6 %copy.17 = f32[128,256]{1,0:T(8,128)} copy(f32[128,256]{1,0:T(8,128)} %get-tuple-element.8) | data formatting | bytes 262144
